TPU v7x, 32 devices: a whole 2x2x4 slice. The times are simulated.
32 devices in a mesh: views: 2 (over y), tiles: 16 (over z, x, core).
Axes of the slice: x: 2, y: 2, z: 4, core: 2. Of those that a mesh axis runs over, the one named last changes fastest.
Arguments:
- linear_point: float32 [59, 8192], P(None, 'tiles'), may hold values from -6 to 6
- right_side: float32 [59, 8192], P(None, 'tiles'), may hold values from -75 to 75
- damping: float32 [59, 8192], P(None, 'tiles'), may hold values from 0.2 to 2
- projection: float32 [2, 59, 16], P('views'), may hold values from -0.75 to 0.75
- pixel_basis: float32 [2, 16, 12, 128], P('views', 'tiles'), may hold values from -1.8 to 1.8
- pixel_weight: float32 [2, 16, 128], P('views', 'tiles'), may hold values from 50 to 500
- depth_order: int32 [2, 16, 512], P('views', 'tiles'), may hold values from 0 to 511, each once within a row
- tile_dest: int32 [2, 1024, 1], P('views', 'tiles'), may hold values from 0 to 15; in each aligned block of 64 rows (0 to 63, 64 to 127, ..., all dimensions but the last counted through in order) at most 4 rows name the same one
- block_depth: int32 [2, 1024], P('views', 'tiles'), may hold values from 0 to 1023, each once within a row
Outputs:
- solution: float32 [59, 8192], P(None, 'tiles')
- residual: float32 [59, 8192], P(None, 'tiles')
Inputs may be any that keep to these rules, and one draw needn't show every extreme that they name: `tile_dest`: each block of one owner in one view names one tile; no tile is named by more than 4 blocks of one owner in one view, a bound that the blocks of some owner reach; every tile is named by some block of every view. `depth_order`: for each view and owner, a permutation of the owner's local Gaussian numbers. `block_depth`: for each view, a permutation of the block numbers.
All inputs are finite; a program needn't handle non-finite values.
Results may differ from a plain program's by a relative error of at most 0.007.
Values sent between devices are 32-bit elements; how exact they have to be, the bound alone decides.
A program may use at most 64 MiB of HBM per device.

v0:
```python
import jax
import jax.numpy as jnp
from jax import lax
from jax.sharding import PartitionSpec as P

ITERS = 2


PRECISE = lax.Precision.HIGHEST
OFFSET = 6.0


def blend(blocks, depth_marks, tile_basis):
    logits = (
        blocks[:, 0, :, None]
        - OFFSET
        + jnp.einsum("skr,kp->srp", blocks[:, 4:, :], tile_basis, precision=PRECISE)
    )
    alphas = jax.nn.sigmoid(logits)
    log_clear = -jax.nn.softplus(logits)
    before = jnp.cumsum(log_clear, axis=1) - log_clear
    colors = jnp.einsum(
        "scr,srp->scp", blocks[:, 1:4, :], alphas * jnp.exp(before), precision=PRECISE
    )
    filled = (depth_marks > 0.0).astype(jnp.float32)
    colors = colors * filled[:, None, None]
    through = jnp.sum(log_clear, axis=1) * filled[:, None]
    earlier = ((depth_marks[None, :] < depth_marks[:, None]) & (depth_marks[None, :] > 0.0)).astype(
        jnp.float32
    )
    ahead = jnp.dot(earlier, through, precision=PRECISE)
    return jnp.einsum("sp,scp->cp", jnp.exp(ahead), colors, precision=PRECISE)


def body(
    linear_point,
    right_side,
    damping,
    projection,
    pixel_basis,
    pixel_weight,
    depth_order,
    tile_dest,
    block_depth,
):
    view_proj = projection[0]
    tile_basis = pixel_basis[0, 0]
    tile_weight = pixel_weight[0, 0]
    local_order = depth_order[0, 0]
    local_dest = tile_dest[0, :, 0]
    local_depth = block_depth[0]
    owners = lax.axis_size("tiles")
    count = local_dest.shape[0]
    gauss_local = local_order.shape[0]
    per_block = gauss_local // count
    capacity = max(2, count // owners)
    slots = owners * capacity
    shared = local_dest[None, :] == local_dest[:, None]
    before = jnp.arange(count)[None, :] < jnp.arange(count)[:, None]
    position = jnp.sum((shared & before).astype(jnp.int32), axis=1)
    slot_of = local_dest * capacity + position
    block_of = jnp.zeros((slots,), jnp.int32).at[slot_of].set(jnp.arange(count, dtype=jnp.int32))
    occupied = jnp.zeros((slots,), jnp.float32).at[slot_of].set(1.0)
    marks_send = (
        jnp.zeros((slots,), jnp.float32).at[slot_of].set(local_depth.astype(jnp.float32) + 1.0)
    )
    inverse = (
        jnp.zeros((gauss_local,), jnp.int32)
        .at[local_order]
        .set(jnp.arange(gauss_local, dtype=jnp.int32))
    )

    def to_slots(vector):
        picked = jnp.take(vector, local_order, axis=1).reshape(vector.shape[0], count, per_block)
        blocks = jnp.einsum("kf,kbr->bfr", view_proj, picked, precision=PRECISE)
        return jnp.take(blocks, block_of, axis=0) * occupied[:, None, None]

    def from_slots(returned):
        blocks = jnp.take(returned, slot_of, axis=0)
        params_sorted = jnp.einsum("kf,bfr->kbr", view_proj, blocks, precision=PRECISE)
        return jnp.take(params_sorted.reshape(view_proj.shape[0], gauss_local), inverse, axis=1)

    primal_send = to_slots(linear_point)

    def apply_normal(vector):
        primal_now, tangent_recv, marks_now = (
            lax.all_to_all(primal_send, "tiles", split_axis=0, concat_axis=0, tiled=True),
            lax.all_to_all(to_slots(vector), "tiles", split_axis=0, concat_axis=0, tiled=True),
            lax.all_to_all(marks_send, "tiles", split_axis=0, concat_axis=0, tiled=True),
        )

        def blend_now(blocks):
            return blend(blocks, marks_now, tile_basis)

        image_tangent = jax.jvp(blend_now, (primal_now,), (tangent_recv,))[1]
        unused_out, pull = jax.vjp(blend_now, primal_now)
        cotangent = pull(image_tangent * tile_weight[None, :])[0]
        returned = lax.all_to_all(cotangent, "tiles", split_axis=0, concat_axis=0, tiled=True)
        return from_slots(returned)

    def squares(vector):
        return lax.psum(jnp.sum(vector * vector), "tiles")

    solution = jnp.zeros_like(right_side)
    residual = right_side
    direction = right_side
    norm_now = squares(residual)
    for iteration in range(ITERS):
        product = lax.psum(apply_normal(direction), "views") + damping * direction
        step_size = norm_now / lax.psum(jnp.sum(direction * product), "tiles")
        solution = solution + step_size * direction
        residual = residual - step_size * product
        norm_next = squares(residual)
        direction = residual + norm_next / norm_now * direction
        norm_now = norm_next
    return (solution, residual)


def solution(mesh):
    in_specs = (
        P(None, "tiles"),
        P(None, "tiles"),
        P(None, "tiles"),
        P("views", None, None),
        P("views", "tiles", None, None),
        P("views", "tiles", None),
        P("views", "tiles", None),
        P("views", "tiles", None),
        P("views", "tiles"),
    )
    out_specs = (P(None, "tiles"), P(None, "tiles"))
    return jax.shard_map(body, mesh=mesh, in_specs=in_specs, out_specs=out_specs, check_vma=False)
```

profile of v0, /device:TPU:0, one launch (start us, length us, event | category | flops | bytes accessed | tf_op | source)
XLA Modules:
  0.0 268.0 jit_solution(1362588183108304653)
XLA Ops:
  8.7 0.8 scatter_custom_fusion.2
  9.5 0.7 all_to_all.27
  10.1 7.4 %all-to-all-start.2 = ((f32[16,4,1]{1,2,0:T(1,128)}), f32[16,4,1]{1,2,0:T(1,128)S(1)}, u32[]{:S(2)}, u32[]{:S(2)}) async-start(f32[16,4,1]{1,2,0:T(1,128)} %bitcast.28), calls=%async_computation.2 | async-start | bytes 16384 | tf_op jit(solution)/shard_map/all_to_all | solution.py:89
  17.5 0.8 scatter_custom_fusion
  19.0 2.4 scatter_custom_fusion.3
  21.5 0.8 scatter_custom_fusion.1
  22.3 1.1 copy.272
  23.6 1.0 gather_fusion.2
  24.6 1.0 gather_fusion
  25.8 0.7 convolution_bitcast_fusion.6
  26.5 0.7 convolution_bitcast_fusion.5
  29.1 0.8 reshape.316
  29.9 0.8 reshape.314
  30.6 6.0 %all-to-all-start = ((f32[16,1,512]{2,1,0:T(1,128)}), f32[16,1,512]{2,1,0:T(1,128)S(1)}, u32[]{:S(2)}, u32[]{:S(2)}) async-start(f32[16,1,512]{2,1,0:T(1,128)} %reshape.316), calls=%async_computation | async-start | bytes 65536 | tf_op jit(solution)/shard_map/all_to_all | solution.py:88
  37.2 0.7 reduce.15
  38.1 5.2 %all-to-all-done = f32[16,1,512]{2,1,0:T(1,128)S(1)} async-done(((f32[16,1,512]{2,1,0:T(1,128)}), f32[16,1,512]{2,1,0:T(1,128)S(1)}, u32[]{:S(2)}, u32[]{:S(2)}) %all-to-all-start) | async-done | bytes 32800 | tf_op jit(solution)/shard_map/all_to_all | solution.py:88
  43.3 3.7 %all-to-all-start.1 = ((f32[16,1,512]{2,1,0:T(1,128)}), f32[16,1,512]{2,1,0:T(1,128)S(1)}, u32[]{:S(2)}, u32[]{:S(2)}) async-start(f32[16,1,512]{2,1,0:T(1,128)} %reshape.314), calls=%async_computation.1 | async-start | bytes 65536 | tf_op jit(solution)/shard_map/all_to_all | solution.py:87
  47.5 0.7 reduce.17
  48.8 4.6 %all-to-all-done.1 = f32[16,1,512]{2,1,0:T(1,128)S(1)} async-done(((f32[16,1,512]{2,1,0:T(1,128)}), f32[16,1,512]{2,1,0:T(1,128)S(1)}, u32[]{:S(2)}, u32[]{:S(2)}) %all-to-all-start.1) | async-done | bytes 32800 | tf_op jit(solution)/shard_map/all_to_all | solution.py:87
  53.4 0.7 reduce.16
  55.5 0.7 fusion.123
  57.0 0.9 fusion.17
  58.3 0.9 multiply_reduce_fusion.3
  59.2 0.9 fusion.6
  63.3 3.6 %convolution_bitcast_fusion.1 = f32[64,12,8]{2,1,0:T(8,128)S(1)} fusion(f32[64,8,128]{2,1,0:T(8,128)S(1)} %get-tuple-element.39, f32[1,1,12,128]{3,1,2,0:T(1,128)S(1)} %copy-done.5), kind=kOutput, calls=%fused_computation.15 | convolution fusion | flops 9437184 | bytes 292864 | tf_op jit(solution)/shard_map/transpose(jvp(skr,kp->srp))/dot_general | solution.py:17
  67.2 0.8 reshape.318
  68.0 3.5 %all-to-all-start.3 = ((f32[16,1,512]{2,1,0:T(1,128)}), f32[16,1,512]{2,1,0:T(1,128)S(1)}, u32[]{:S(2)}, u32[]{:S(2)}) async-start(f32[16,1,512]{2,1,0:T(1,128)} %reshape.318), calls=%async_computation.3 | async-start | bytes 65536 | tf_op jit(solution)/shard_map/all_to_all | solution.py:98
  71.5 6.5 %all-to-all-done.3 = f32[16,1,512]{2,1,0:T(1,128)S(1)} async-done(((f32[16,1,512]{2,1,0:T(1,128)}), f32[16,1,512]{2,1,0:T(1,128)S(1)}, u32[]{:S(2)}, u32[]{:S(2)}) %all-to-all-start.3) | async-done | bytes 32800 | tf_op jit(solution)/shard_map/all_to_all | solution.py:98
  78.1 0.7 reduce.18
  80.2 1.0 gather_fusion.5
  82.1 18.8 %all-reduce.10.cloned.1.call-done = f32[59,512]{1,0:T(8,128)} async-done(((f32[59,512]{1,0:T(8,128)}), f32[59,512]{1,0:T(8,128)}) %all-reduce.10.cloned.1.call-update) | async-done | bytes 120848 | tf_op jit(solution)/shard_map/psum | solution.py:109
  101.0 1.7 multiply_reduce_fusion.6
  102.7 33.3 %all-reduce.6 = (f32[]{:T(128)}, f32[]{:T(128)}) all-reduce(f32[]{:T(128)} %get-tuple-element.27, f32[]{:T(128)} %get-tuple-element.26), channel_id=1, replica_groups=mesh['views'=2,'tiles'=16] {'tiles'}, use_global_device_ids=true, to_apply=%region_1.0 | all-reduce | flops 2 | bytes 16 | tf_op jit(solution)/shard_map/psum | solution.py:102
  137.9 30.4 %psum.45 = f32[]{:T(128)} all-reduce(f32[]{:T(128)} %get-tuple-element.34), channel_id=1, replica_groups=mesh['views'=2,'tiles'=16] {'tiles'}, use_global_device_ids=true, to_apply=%region_19.24 | all-reduce | flops 1 | bytes 8 | tf_op jit(solution)/shard_map/psum | solution.py:102
  169.8 1.0 gather_fusion.6
  170.9 0.7 convolution_bitcast_fusion.4
  172.8 9.2 %all_to_all.39 = f32[16,1,512]{2,1,0:T(1,128)S(1)} all-to-all(f32[16,1,512]{2,1,0:T(1,128)S(1)} %reshape.320), channel_id=1, replica_groups=mesh['views'=2,'tiles'=16] {'tiles'}, dimensions={0} | all-to-all | bytes 65536 | tf_op jit(solution)/shard_map/all_to_all | solution.py:88
  182.0 0.7 reduce.19
  182.9 0.9 fusion.13
  185.4 0.9 fusion.7
  188.8 3.6 %convolution_bitcast_fusion = f32[64,12,8]{2,1,0:T(8,128)S(1)} fusion(f32[64,8,128]{2,1,0:T(8,128)S(1)} %get-tuple-element.31, f32[1,1,12,128]{3,1,2,0:T(1,128)S(1)} %copy-done.5), kind=kOutput, calls=%fused_computation.14 | convolution fusion | flops 9437184 | bytes 292864 | tf_op jit(solution)/shard_map/transpose(jvp(skr,kp->srp))/dot_general | solution.py:17
  192.9 9.2 %all_to_all.40 = f32[16,1,512]{2,1,0:T(1,128)S(1)} all-to-all(f32[16,1,512]{2,1,0:T(1,128)S(1)} %reshape.322), channel_id=1, replica_groups=mesh['views'=2,'tiles'=16] {'tiles'}, dimensions={0} | all-to-all | bytes 65536 | tf_op jit(solution)/shard_map/all_to_all | solution.py:98
  202.1 0.7 reduce.20
  204.3 1.0 gather_fusion.9
  206.2 17.9 %all-reduce.12.cloned.1.call-done = f32[59,512]{1,0:T(8,128)} async-done(((f32[59,512]{1,0:T(8,128)}), f32[59,512]{1,0:T(8,128)}) %all-reduce.12.cloned.1.call-update) | async-done | bytes 120848 | tf_op jit(solution)/shard_map/psum | solution.py:109
  224.1 1.6 multiply_reduce_fusion.4
  225.7 33.3 %psum.47 = f32[]{:T(128)} all-reduce(f32[]{:T(128)} %multiply_reduce_fusion.4), channel_id=1, replica_groups=mesh['views'=2,'tiles'=16] {'tiles'}, use_global_device_ids=true, to_apply=%region_28.33 | all-reduce | flops 1 | bytes 8 | tf_op jit(solution)/shard_map/psum | solution.py:110
  260.4 0.8 multiply_subtract_fusion
  (115 shorter events, 23.3 us)
Async XLA Ops:
  7.2 18.6 %copy-start = (f32[1,59,16]{1,2,0:T(8,128)S(1)}, f32[1,59,16]{1,2,0:T(8,128)}, u32[]{:S(2)}) copy-start(f32[1,59,16]{1,2,0:T(8,128)} %param.19) | copy-start | bytes 11332
  7.2 0.7 copy-start.8
  8.0 0.7 copy-start.9
  10.1 20.5 %all-to-all-start.2 = ((f32[16,4,1]{1,2,0:T(1,128)}), f32[16,4,1]{1,2,0:T(1,128)S(1)}, u32[]{:S(2)}, u32[]{:S(2)}) async-start(f32[16,4,1]{1,2,0:T(1,128)} %bitcast.28), calls=%async_computation.2 | async-start | bytes 16384 | tf_op jit(solution)/shard_map/all_to_all | solution.py:89
  18.3 0.7 copy-start.6
  22.3 1.1 copy-start.1
  30.6 12.6 %all-to-all-start = ((f32[16,1,512]{2,1,0:T(1,128)}), f32[16,1,512]{2,1,0:T(1,128)S(1)}, u32[]{:S(2)}, u32[]{:S(2)}) async-start(f32[16,1,512]{2,1,0:T(1,128)} %reshape.316), calls=%async_computation | async-start | bytes 65536 | tf_op jit(solution)/shard_map/all_to_all | solution.py:88
  43.3 10.1 %all-to-all-start.1 = ((f32[16,1,512]{2,1,0:T(1,128)}), f32[16,1,512]{2,1,0:T(1,128)S(1)}, u32[]{:S(2)}, u32[]{:S(2)}) async-start(f32[16,1,512]{2,1,0:T(1,128)} %reshape.314), calls=%async_computation.1 | async-start | bytes 65536 | tf_op jit(solution)/shard_map/all_to_all | solution.py:87
  54.4 0.7 copy-start.5
  60.1 0.7 copy-start.7
  68.0 10.1 %all-to-all-start.3 = ((f32[16,1,512]{2,1,0:T(1,128)}), f32[16,1,512]{2,1,0:T(1,128)S(1)}, u32[]{:S(2)}, u32[]{:S(2)}) async-start(f32[16,1,512]{2,1,0:T(1,128)} %reshape.318), calls=%async_computation.3 | async-start | bytes 65536 | tf_op jit(solution)/shard_map/all_to_all | solution.py:98
  71.5 29.5 %all-reduce.10.cloned.1.call-start = ((), (), s32[]{:S(2)}) async-start(), calls=%async_computation.6 | async-start | bytes 262144 | tf_op jit(solution)/shard_map/psum | solution.py:109
  82.1 18.9 %copy-start.2 = (f32[59,512]{1,0:T(8,128)S(1)}, f32[59,512]{1,0:T(8,128)}, u32[]{:S(2)}) copy-start(f32[59,512]{1,0:T(8,128)} %param.18) | copy-start | bytes 362500
  82.1 142.0 %all-reduce.12.cloned.1.call-start = ((), (), s32[]{:S(2)}) async-start(), calls=%async_computation.7 | async-start | bytes 262144 | tf_op jit(solution)/shard_map/psum | solution.py:109
  101.0 36.3 %copy-start.3 = (f32[59,512]{1,0:T(8,128)S(1)}, f32[59,512]{1,0:T(8,128)}, u32[]{:S(2)}) copy-start(f32[59,512]{1,0:T(8,128)} %all-reduce.10.cloned.1.call-done) | copy-start | bytes 362500
  224.1 36.3 %copy-start.4 = (f32[59,512]{1,0:T(8,128)S(1)}, f32[59,512]{1,0:T(8,128)}, u32[]{:S(2)}) copy-start(f32[59,512]{1,0:T(8,128)} %all-reduce.12.cloned.1.call-done) | copy-start | bytes 362500
Sparse Core Ops, SparseCore 0:
  82.2 18.7 all-reduce.9
  206.3 17.7 all-reduce.11
where the time goes:
time: 269 us; the launch traced here: 268 us
  blocking collectives  115 us (43%)
  waiting for transfers between devices  53.1 us (20%)
  local copies, waits for them, and re-layouts  25.3 us (9%)
  starting transfers between devices  20.6 us (8%)
  matrix products  20 us (7%)
  between operations  18.7 us (7%)
  other arithmetic  14.8 us (6%)
    psum x2, blocking collectives, squares(): return lax.psum(jnp.sum(vector * vector), 'tiles')  63.7 us
    psum x2, waiting for transfers between devices, body(): product = lax.psum(apply_normal(direction), 'views') + damping * direction  36.7 us
    psum x1, blocking collectives, body(): step_size = norm_now / lax.psum(jnp.sum(direction * product), 'tiles')  33.3 us
    all_to_all x1, blocking collectives, apply_normal(): lax.all_to_all(to_slots(vector), 'tiles', split_axis=0, concat_axis=0, ti...  9.2 us
    all_to_all x1, blocking collectives, apply_normal(): lax.all_to_all(cotangent, 'tiles', split_axis=0, concat_axis=0, tiled=True)  9.2 us
    dot_general x5, matrix products, blend(): jnp.einsum('skr,kp->srp', blocks[:, 4:, :], tile_basis, precision=PRECISE)  8.89 us
    unnamed x33, local copies, waits for them, and re-layouts  7.83 us
    all_to_all x1, starting transfers between devices, apply_normal(): lax.all_to_all(marks_send, 'tiles', split_axis=0, concat_axis=0, tiled=True)  7.36 us
  transfers between devices with their start and end apart: 6, of which 5 were waited for; matrix products, arithmetic and copies ran while one was open for 6% of the time, Pallas kernels for 0%

commit v1 on v0

v1 whole, which is shorter than its diff:
```python
import functools

import jax
import jax.numpy as jnp
from jax import lax
from jax.experimental import pallas as pl
from jax.experimental.pallas import tpu as pltpu
from jax.sharding import PartitionSpec as P

MESH = pl.DeviceIdType.MESH
F32 = jnp.float32
BF16 = jnp.bfloat16
FEATS = 16
OFFSET = 6.0


def dot16(a, b, dims=((1,), (0,))):
    return lax.dot_general(a, b, (dims, ((), ())), preferred_element_type=F32)


def split(x):
    high = x.astype(BF16)
    return high, (x - high.astype(F32)).astype(BF16)


def stacked(x):
    return jnp.concatenate(split(x), axis=0)


def halves_sum(x):
    rows = x.shape[0] // 2
    return x[:rows] + x[rows:]


def pick(x, onehot, dims=((1,), (0,))):
    return halves_sum(dot16(stacked(x), onehot, dims))


def pick_left(twice, x):
    return dot16(twice, stacked(x))


def small_dot(a, b):
    high, low = split(b)
    left = stacked(a)
    return halves_sum(dot16(left, high)) + dot16(left[: a.shape[0]], low)


def wide_dot(a, pair):
    return halves_sum_wide(dot16(stacked(a), pair))


def halves_sum_wide(x):
    rows, lanes = x.shape[0] // 2, x.shape[1] // 2
    return x[:rows, :lanes] + x[rows:, :lanes] + x[:rows, lanes:]


def paired(x):
    return jnp.concatenate(split(x), axis=1)


def wide_dot_t(a, pair):
    high, low = split(a)
    left = jnp.concatenate(
        [
            jnp.concatenate([high, high], axis=1),
            jnp.concatenate([low, jnp.zeros_like(low)], axis=1),
        ],
        axis=0,
    )
    return halves_sum(dot16(left, pair, ((1,), (1,))))


def three_a(x):
    high, low = split(x)
    return jnp.concatenate([high, high, low], axis=0)


def three_b(x):
    high, low = split(x)
    return jnp.concatenate([high, low, high], axis=0)


def iota(shape, axis):
    return lax.broadcasted_iota(jnp.int32, shape, axis)


def total(x):
    return jnp.sum(jnp.sum(x, axis=0, keepdims=True), axis=1, keepdims=True)


def swap_blocks(x, width):
    groups = 128 // width
    depth = FEATS // groups
    rows, lanes = iota(x.shape, 0), iota(x.shape, 1)
    bit = 1
    while bit < groups:
        up, over = depth * bit, width * bit
        row_bit = (rows // up) % 2
        lane_bit = (lanes // over) % 2
        down = pltpu.roll(pltpu.roll(x, FEATS - up, 0), over, 1)
        back = pltpu.roll(pltpu.roll(x, up, 0), 128 - over, 1)
        x = jnp.where(row_bit == lane_bit, x, jnp.where(lane_bit == 1, down, back))
        bit *= 2
    return x


def kernel(
    views,
    tiles,
    *refs,
):
    my_view = lax.axis_index("views")
    me = lax.axis_index("tiles")
    flat = my_view * tiles + me
    everyone = views * tiles
    inputs, refs = refs[:9], refs[9:]
    sol_ref, res_ref, onehot, xbuf = refs[:4]
    f1_send, f1_recv, b1_send, b1_recv, f2_send, f2_recv, b2_send, b2_recv = refs[4:12]
    held, (send_sem, recv_sem, in_sem) = refs[12:21], refs[21:]
    lp_ref, rs_ref, dm_ref, proj_ref, basis_ref, weight_ref, order_ref, dest_ref, depth_ref = held
    fetches = [
        pltpu.make_async_copy(inputs[i], held[i], in_sem.at[i]) for i in range(9)
    ]
    for i in (6, 7, 8, 3, 1, 0, 2, 4, 5):
        fetches[i].start()
    count = dest_ref.shape[1]
    gauss = order_ref.shape[1]
    params = rs_ref.shape[0]
    per = gauss // count
    capacity = max(2, count // tiles)
    width = per * capacity
    places = tiles * width
    blocks = places // 128
    groups = 128 // width
    depth = FEATS // groups

    barrier = pltpu.get_barrier_semaphore()

    def greet(k, carry):
        other = lax.rem(flat + k, everyone)
        pl.semaphore_signal(
            barrier, inc=1, device_id=(other // tiles, lax.rem(other, tiles)), device_id_type=MESH
        )
        return carry

    lax.fori_loop(1, everyone, greet, 0)

    eye = iota((count, count), 0) == iota((count, count), 1)
    for i in (6, 7, 8):
        fetches[i].wait()
    dest_row = dest_ref[...].astype(F32)
    dest = jnp.sum(jnp.where(eye, dest_row, 0.0), axis=1, keepdims=True)
    earlier = iota((count, count), 1) < iota((count, count), 0)
    position = jnp.sum(
        jnp.where((dest_row == dest) & earlier, 1.0, 0.0), axis=1, keepdims=True
    )
    slot = dest * float(capacity) + position
    mark = jnp.sum(jnp.where(eye, depth_ref[...].astype(F32), 0.0), axis=1, keepdims=True) + 1.0
    order = order_ref[...]
    own = iota((count, gauss), 1) // per == iota((count, gauss), 0)
    high = jnp.where(own, (order // 256).astype(F32), 0.0)
    low = jnp.where(own, (order % 256).astype(F32), 0.0)
    spread = (
        iota((gauss, 128), 0) % per == (iota((gauss, 128), 1) % width) // capacity
    ).astype(F32).astype(BF16)
    listed = dot16(jnp.concatenate([high, low], axis=0).astype(BF16), spread)
    listed = listed[:count] * 256.0 + listed[count:] + 1.0
    ids, marks = [], []
    for k in range(blocks):
        lane = iota((count, 128), 1) + k * 128
        wanted = (lane // width) * capacity + lane % capacity
        here = slot == wanted.astype(F32)
        ids.append(jnp.sum(jnp.where(here, listed, 0.0), axis=0, keepdims=True) - 1.0)
        marks.append(jnp.sum(jnp.where(here, mark, 0.0), axis=0, keepdims=True))

    def place_matrix(rows):
        numbers = iota((gauss, 128), 0).astype(F32)
        return jnp.concatenate(
            [(numbers == row).astype(F32).astype(BF16) for row in rows], axis=1
        )

    mine = place_matrix(ids)
    onehot[my_view] = mine
    for i in (3, 1, 0, 2, 4, 5):
        fetches[i].wait()
    proj = proj_ref[...]
    xbuf[my_view, 0:FEATS, 0:params] = proj
    for k in range(blocks):
        xbuf[my_view, FEATS + k : FEATS + 1 + k, :] = ids[k]

    right = rs_ref[...]
    damp = dm_ref[...]
    u_both = jnp.concatenate(
        [small_dot(proj, lp_ref[...]), small_dot(proj, right)], axis=0
    )
    u_both = pick(u_both, mine)
    damped = damp * right
    lane = iota((1, 128), 1)

    def put(buf, start, parts):
        for k in range(blocks):
            for row in range(FEATS):
                buf[k * groups + row // depth, start + row % depth] = parts[k][row : row + 1]

    def swapped(u):
        return [swap_blocks(u[:, k * 128 : k * 128 + 128], width) for k in range(blocks)]

    put(f1_send, 0, swapped(u_both[:FEATS]))
    put(f1_send, depth, swapped(u_both[FEATS:]))
    sums = jnp.where(lane == width, total(right * right), 0.0) + jnp.where(
        lane == width + 1, total(damped * right), 0.0
    )
    top = iota((FEATS, 128), 0) == 0
    for k in range(blocks):
        ranks = swap_blocks(jnp.where(top, marks[k], 0.0), width)
        for j in range(groups):
            f1_send[k * groups + j, 2 * depth] = ranks[j * depth : j * depth + 1] + sums

    pl.semaphore_wait(barrier, everyone - 1)

    def send(src, dst, view, tile, sem):
        return pltpu.make_async_remote_copy(
            src_ref=src,
            dst_ref=dst,
            send_sem=send_sem.at[sem],
            recv_sem=recv_sem.at[sem],
            device_id=(view, tile),
            device_id_type=MESH,
        )

    def to_tiles(src, dst, sem):
        def step(k, carry):
            other = lax.rem(me + k, tiles)
            send(src.at[other], dst.at[me], my_view, other, sem).start()
            return carry

        lax.fori_loop(1, tiles, step, 0)
        dst[me] = src[me]

    def to_owners(src, dst, sem):
        def step(k, carry):
            other = lax.rem(flat + k, everyone)
            tile = lax.rem(other, tiles)
            send(src.at[tile], dst.at[flat], other // tiles, tile, sem).start()
            return carry

        lax.fori_loop(1, everyone, step, 0)
        dst[flat] = src[me]

    def landed(dst, number, sem):
        whole = dst.at[pl.ds(0, number)]
        send(whole, whole, my_view, me, sem).wait_recv()

    def left(src, number, sem):
        whole = src.at[pl.ds(0, number)]
        send(whole, whole, my_view, me, sem).wait_send()

    to_tiles(f1_send, f1_recv, 1)
    for k in range(1, views):
        send(xbuf.at[my_view], xbuf.at[my_view], lax.rem(my_view + k, views), me, 0).start()

    basis = jnp.concatenate(
        [jnp.ones((1, 128), F32), jnp.zeros((3, 128), F32)]
        + [basis_ref[i] for i in range(FEATS - 4)],
        axis=0,
    )
    basis3 = three_b(basis)
    weight = weight_ref[...]
    color_row = (iota((FEATS, 128), 0) >= 1) & (iota((FEATS, 128), 0) <= 3)

    landed(f1_recv, tiles - 1, 1)

    def gathered(buf, first, start):
        out = []
        for k in range(blocks):
            rows = [
                buf[first + k * groups + row // depth, start + row % depth] for row in range(FEATS)
            ]
            out.append(swap_blocks(jnp.concatenate(rows, axis=0), width))
        return out

    def turned(parts):
        return jnp.concatenate([part.T for part in parts], axis=0)

    def turned3(parts):
        return turned([three_a(part).astype(F32) for part in parts]).astype(BF16)

    primal_parts = gathered(f1_recv, 0, 0)
    u0 = jnp.concatenate(primal_parts, axis=1)
    u0_t = turned3(primal_parts)
    ranks = []
    for k in range(blocks):
        rows = []
        for j in range(groups):
            row = f1_recv[k * groups + j, 2 * depth]
            rows.append(jnp.where(lane < width, row, 0.0))
            rows.append(jnp.zeros((depth - 1, 128), F32))
        ranks.append(swap_blocks(jnp.concatenate(rows, axis=0), width))
    marks_t = turned(ranks)[:, 0:1]

    def lanes_total(buf, row, number):
        out = buf[0, row]
        for t in range(1, number):
            out = out + buf[t, row]
        return out

    sums = lanes_total(f1_recv, 2 * depth, tiles)
    rr, rdr = sums[:, width : width + 1], sums[:, width + 1 : width + 2]

    halves = 8 // capacity
    steps = width // 8
    small = tiles * 8
    sub = iota((tiles * steps, 8, 128), 1)

    def scan(x):
        x = x.reshape(tiles * steps, 8, 128)
        through = inner = x
        step = 1
        while step < halves:
            shift = step * capacity
            inner = inner + jnp.where(sub >= shift, pltpu.roll(inner, shift, 1), 0.0)
            through = through + pltpu.roll(through, shift, 1)
            step *= 2
        before = inner - x
        through = through.reshape(tiles, steps, 8, 128)
        before = before.reshape(tiles, steps, 8, 128)
        run = jnp.zeros((tiles, 8, 128), F32)
        out = []
        for i in range(steps):
            out.append(before[:, i] + run)
            run = run + through[:, i]
        return jnp.stack(out, axis=1), run

    def wide(x):
        return x.reshape(tiles, 1, 8, 128)

    def full(x):
        return x.reshape(tiles, steps, 8, 128)

    mark_col = marks_t.reshape(tiles, width, 1)[:, 0:8, :].reshape(small, 1)
    square = (small, small)
    mark_row = jnp.sum(
        jnp.where(iota(square, 0) == iota(square, 1), mark_col, 0.0), axis=0, keepdims=True
    )
    first = (iota(square, 1) % 8) < capacity
    ahead = (first & (mark_row < mark_col) & (mark_row > 0.0)).astype(F32).astype(BF16)
    behind = (first & (mark_row > mark_col)).astype(F32).astype(BF16)
    ahead = jnp.concatenate([ahead, ahead], axis=1)
    behind = jnp.concatenate([behind, behind], axis=1)

    z = dot16(u0_t, basis3) - OFFSET
    filled = marks_t > 0.0
    tail = jnp.exp(-jnp.abs(z))
    alpha = jnp.where(filled, jnp.where(z >= 0.0, 1.0, tail) / (1.0 + tail), 0.0)
    clear = jnp.where(filled, -(jnp.maximum(z, 0.0) + jnp.log1p(tail)), 0.0)
    before, through = scan(clear)
    before = before + wide(pick_left(ahead, through.reshape(small, 128)))
    visible = full(alpha) * jnp.exp(before)
    visible_pair = paired(visible.reshape(places, 128))
    alpha = full(alpha)
    rest = 1.0 - alpha

    def image_tangent(parts):
        du = jnp.concatenate(parts, axis=1)
        dz = full(dot16(turned3(parts), basis3))
        before, through = scan(-alpha * dz)
        before = before + wide(pick_left(ahead, through.reshape(small, 128)))
        moved = visible * (rest * dz + before)
        return wide_dot(du, visible_pair) + wide_dot(u0, paired(moved.reshape(places, 128)))

    def cotangent(image, buf):
        image = jnp.where(color_row, image, 0.0)
        pull = image * weight
        energy = jnp.broadcast_to(total(pull * image), (1, 128))
        h = full(dot16(u0_t, three_b(pull))) * visible
        before, through = scan(h)
        later = through + pick_left(behind, through.reshape(small, 128)).reshape(tiles, 8, 128)
        z_bar = h * rest - alpha * (wide(later) - before - h)
        u_bar = wide_dot_t(basis, paired(z_bar.reshape(places, 128))) + wide_dot_t(
            pull, visible_pair
        )
        put(buf, 0, swapped(u_bar))
        for t in range(tiles):
            buf[t, depth] = energy

    def parameters(buf):
        left, right = [], []
        for v in range(views):
            u_bar = jnp.concatenate(gathered(buf, v * tiles, 0), axis=1)
            left.append(three_a(xbuf[v, 0:FEATS, :]))
            right.append(three_b(pick(u_bar, onehot[v], ((1,), (1,)))))
        out = dot16(
            jnp.concatenate(left, axis=0), jnp.concatenate(right, axis=0), ((0,), (0,))
        )
        return out[:params], lanes_total(buf, depth, everyone)[:, 0:1]

    image1 = image_tangent(gathered(f1_recv, 0, depth))
    cotangent(image1, b1_send)
    to_owners(b1_send, b1_recv, 2)

    if views > 1:
        landed(xbuf, views - 1, 0)
    for k in range(1, views):
        other = lax.rem(my_view + k, views)
        onehot[other] = place_matrix(
            [xbuf[other, FEATS + b : FEATS + 1 + b, :] for b in range(blocks)]
        )

    landed(b1_recv, everyone - 1, 2)
    product, energy = parameters(b1_recv)
    product = product + damped
    step1 = rr / (energy + rdr)
    residual = right - step1 * product
    put(f2_send, 0, swapped(pick(small_dot(proj, residual), mine)))
    sums = (
        jnp.where(lane == 0, total(residual * residual), 0.0)
        + jnp.where(lane == 1, total(damp * residual * residual), 0.0)
        + jnp.where(lane == 2, total(damped * residual), 0.0)
    )
    for t in range(tiles):
        f2_send[t, depth] = sums
    to_tiles(f2_send, f2_recv, 3)

    landed(f2_recv, tiles - 1, 3)
    sums = lanes_total(f2_recv, depth, tiles)
    rr1, sds, sdr = sums[:, 0:1], sums[:, 1:2], sums[:, 2:3]
    beta = rr1 / rr
    image2 = image_tangent(gathered(f2_recv, 0, 0)) + beta * image1
    cotangent(image2, b2_send)
    to_owners(b2_send, b2_recv, 4)

    direction = residual + beta * right
    landed(b2_recv, everyone - 1, 4)
    product, energy = parameters(b2_recv)
    product = product + damp * direction
    step2 = rr1 / (energy + sds + 2.0 * beta * sdr + beta * beta * rdr)
    sol_ref[...] = step1 * right + step2 * direction
    res_ref[...] = residual - step2 * product

    if views > 1:
        left(xbuf, views - 1, 0)
    left(f1_recv, tiles - 1, 1)
    left(b1_recv, everyone - 1, 2)
    left(f2_recv, tiles - 1, 3)
    left(b2_recv, everyone - 1, 4)


def solution(mesh):
    views, tiles = mesh.shape["views"], mesh.shape["tiles"]

    def body(*args):
        linear_point, right_side, damping, proj, basis, weight, order, dest, depths = args
        gauss, count = order.shape[2], dest.shape[1]
        capacity = max(2, count // tiles)
        width = gauss // count * capacity
        depth = FEATS * width // 128
        args = (
            linear_point,
            right_side,
            damping,
            jnp.swapaxes(proj[0], 0, 1),
            jnp.swapaxes(basis[0], 0, 1),
            weight[0],
            order[0],
            dest.reshape(1, count),
            depths,
        )
        shape = jax.ShapeDtypeStruct(linear_point.shape, F32)
        vmem = pl.BlockSpec(memory_space=pltpu.VMEM)
        first, later = 2 * depth + 1, depth + 1
        return pl.pallas_call(
            functools.partial(kernel, views, tiles),
            out_shape=(shape, shape),
            in_specs=[pl.BlockSpec(memory_space=pltpu.HBM)] * 9,
            out_specs=(vmem, vmem),
            scratch_shapes=[
                pltpu.VMEM((views, gauss, tiles * width), BF16),
                pltpu.VMEM((views, FEATS + 8, 128), F32),
                pltpu.VMEM((tiles, first, 1, 128), F32),
                pltpu.VMEM((tiles, first, 1, 128), F32),
                pltpu.VMEM((tiles, later, 1, 128), F32),
                pltpu.VMEM((views * tiles, later, 1, 128), F32),
                pltpu.VMEM((tiles, later, 1, 128), F32),
                pltpu.VMEM((tiles, later, 1, 128), F32),
                pltpu.VMEM((tiles, later, 1, 128), F32),
                pltpu.VMEM((views * tiles, later, 1, 128), F32),
            ]
            + [pltpu.VMEM(arg.shape, arg.dtype) for arg in args]
            + [
                pltpu.SemaphoreType.DMA((5,)),
                pltpu.SemaphoreType.DMA((5,)),
                pltpu.SemaphoreType.DMA((9,)),
            ],
            compiler_params=pltpu.CompilerParams(
                collective_id=0, has_side_effects=True, vmem_limit_bytes=63 * 1024 * 1024
            ),
        )(*args)

    in_specs = (
        P(None, "tiles"),
        P(None, "tiles"),
        P(None, "tiles"),
        P("views", None, None),
        P("views", "tiles", None, None),
        P("views", "tiles", None),
        P("views", "tiles", None),
        P("views", "tiles", None),
        P("views", "tiles"),
    )
    out_specs = (P(None, "tiles"), P(None, "tiles"))
    return jax.shard_map(body, mesh=mesh, in_specs=in_specs, out_specs=out_specs, check_vma=False)
```

time: 269 us -> 34 us (0.13)
  blocking collectives: 115 us -> 0 us
  waiting for transfers between devices: 53.1 us -> 0 us
  Pallas kernels: 0 us -> 30.9 us
  local copies, waits for them, and re-layouts: 25.3 us -> 2.26 us
  starting transfers between devices: 20.6 us -> 0 us
  matrix products: 20 us -> 0 us
  between operations: 18.7 us -> 0.65 us
  other arithmetic: 14.8 us -> 0 us
    psum x3 -> x0, blocking collectives: 97 us -> none  [the longest x2 63.7 us: squares(): return lax.psum(jnp.sum(vector * vector), 'tiles')]
    psum x2 -> x0, waiting for transfers between devices: 36.7 us -> none  [body(): product = lax.psum(apply_normal(direction), 'views') + damping * direction]
    pallas_call x0 -> x1, Pallas kernels: none -> 30.9 us  [body(): pl.pallas_call(functools.partial(kernel, views, tiles), out_shape=(shape,...]
    all_to_all x4 -> x0, starting transfers between devices: 20.5 us -> none  [the longest x1 7.36 us: apply_normal(): lax.all_to_all(marks_send, 'tiles', split_axis=0, concat_axis=0, tiled=True)]
    dot_general x24 -> x0, matrix products: 20 us -> none  [the longest x5 8.89 us: blend(): jnp.einsum('skr,kp->srp', blocks[:, 4:, :], tile_basis, precision=PRECISE)]
    all_to_all x2 -> x0, blocking collectives: 18.4 us -> none  [the longest x1 9.2 us: apply_normal(): lax.all_to_all(to_slots(vector), 'tiles', split_axis=0, concat_axis=0, ti...]
    all_to_all x4 -> x0, waiting for transfers between devices: 16.4 us -> none  [the longest x1 6.53 us: apply_normal(): lax.all_to_all(cotangent, 'tiles', split_axis=0, concat_axis=0, tiled=True)]
    gather x12 -> x0, local copies, waits for them, and re-layouts: 8.59 us -> none  [the longest x3 3.11 us: to_slots(): jnp.take(vector, local_order, axis=1)]
  transfers between devices with their start and end apart: 6 -> 0, of which waited for: 5 -> 0; matrix products, arithmetic and copies ran while one was open for 6% -> 0% of each run, Pallas kernels for 0% -> 0%
where the time goes in v1:
time: 34 us; the launch traced here: 33.8 us
  Pallas kernels  30.9 us (91%)
  local copies, waits for them, and re-layouts  2.26 us (7%)
  between operations  0.65 us (2%)
    pallas_call x1, Pallas kernels, body(): pl.pallas_call(functools.partial(kernel, views, tiles), out_shape=(shape,...  30.9 us
    unnamed x4, local copies, waits for them, and re-layouts  2.26 us

profile of v1, /device:TPU:0, one launch (start us, length us, event | category | flops | bytes accessed | tf_op | source)
XLA Modules:
  0.0 33.8 jit_solution(4894853116411124201)
XLA Ops:
  0.6 30.9 %shard_map.104 = (f32[59,512]{1,0:T(8,128)}, f32[59,512]{1,0:T(8,128)}) custom-call(f32[59,512]{1,0:T(8,128)} %refs_0_.1, f32[59,512]{1,0:T(8,128)} %refs_1_.1, f32[59,512]{1,0:T(8,128)} %refs_2_.1, f32[16,59]{1,0:T(8,128)} %bitcast.7, f32[12,1,128]{2,1,0:T(1,128)} %bitcast.8, f32[1,128]{1,0:T(1,128)} %bitcast.10, s32[1,512]{1,0:T(1,128)} %bitcast.9, ...), custom_call_target="tpu_custom_call" | custom-call | tf_op jit(solution)/shard_map/pallas_call | solution.py:472
  31.5 0.0 copy-start
  31.5 1.6 %copy.13 = f32[59,512]{1,0:T(8,128)} copy(f32[59,512]{1,0:T(8,128)} %get-tuple-element.4) | data formatting | bytes 241664
  33.1 0.0 copy-done
  33.2 0.7 %copy.14 = f32[59,512]{1,0:T(8,128)} copy(f32[59,512]{1,0:T(8,128)S(1)} %copy-done) | data formatting | bytes 241664
Async XLA Ops:
  31.5 1.6 %copy-start = (f32[59,512]{1,0:T(8,128)S(1)}, f32[59,512]{1,0:T(8,128)}, u32[]{:S(2)}) copy-start(f32[59,512]{1,0:T(8,128)} %get-tuple-element.5) | copy-start | bytes 362500

commit v2 on v1

--- a/solution.py
+++ b/solution.py
@@ -115,9 +115,9 @@
     flat = my_view * tiles + me
     everyone = views * tiles
     inputs, refs = refs[:9], refs[9:]
-    sol_ref, res_ref, onehot, xbuf = refs[:4]
-    f1_send, f1_recv, b1_send, b1_recv, f2_send, f2_recv, b2_send, b2_recv = refs[4:12]
-    held, (send_sem, recv_sem, in_sem) = refs[12:21], refs[21:]
+    res_ref, change_ref, coef1_ref, coef2_ref, onehot, xbuf = refs[:6]
+    f1_send, f1_recv, b1_send, b1_recv, f2_send, f2_recv, b2_send, b2_recv = refs[6:14]
+    held, (send_sem, recv_sem, in_sem) = refs[14:23], refs[23:]
     lp_ref, rs_ref, dm_ref, proj_ref, basis_ref, weight_ref, order_ref, dest_ref, depth_ref = held
     fetches = [
         pltpu.make_async_copy(inputs[i], held[i], in_sem.at[i]) for i in range(9)
@@ -135,6 +135,13 @@
     groups = 128 // width
     depth = FEATS // groups
 
+    def each(low, high, step):
+        if high <= 32:
+            for k in range(low, high):
+                step(k, 0)
+        else:
+            lax.fori_loop(low, high, step, 0)
+
     barrier = pltpu.get_barrier_semaphore()
 
     def greet(k, carry):
@@ -144,7 +151,7 @@
         )
         return carry
 
-    lax.fori_loop(1, everyone, greet, 0)
+    each(1, everyone, greet)
 
     eye = iota((count, count), 0) == iota((count, count), 1)
     for i in (6, 7, 8):
@@ -235,7 +242,7 @@
             send(src.at[other], dst.at[me], my_view, other, sem).start()
             return carry
 
-        lax.fori_loop(1, tiles, step, 0)
+        each(1, tiles, step)
         dst[me] = src[me]
 
     def to_owners(src, dst, sem):
@@ -245,7 +252,7 @@
             send(src.at[tile], dst.at[flat], other // tiles, tile, sem).start()
             return carry
 
-        lax.fori_loop(1, everyone, step, 0)
+        each(1, everyone, step)
         dst[flat] = src[me]
 
     def landed(dst, number, sem):
@@ -311,32 +318,49 @@
     halves = 8 // capacity
     steps = width // 8
     small = tiles * 8
-    sub = iota((tiles * steps, 8, 128), 1)
+    some = 4
+    chunks = tiles // some
+    rows = some * width
+    sub = iota((some * steps, 8, 128), 1)
 
     def scan(x):
-        x = x.reshape(tiles * steps, 8, 128)
-        through = inner = x
-        step = 1
-        while step < halves:
-            shift = step * capacity
-            inner = inner + jnp.where(sub >= shift, pltpu.roll(inner, shift, 1), 0.0)
-            through = through + pltpu.roll(through, shift, 1)
-            step *= 2
-        before = inner - x
-        through = through.reshape(tiles, steps, 8, 128)
-        before = before.reshape(tiles, steps, 8, 128)
-        run = jnp.zeros((tiles, 8, 128), F32)
-        out = []
-        for i in range(steps):
+        x = x.reshape(some * steps, 8, 128)
+        if halves == 2:
+            moved = pltpu.roll(x, capacity, 1)
+            before = jnp.where(sub >= capacity, moved, 0.0)
+            through = x + moved
+        else:
+            through = inner = x
+            step = 1
+            while step < halves:
+                shift = step * capacity
+                inner = inner + jnp.where(sub >= shift, pltpu.roll(inner, shift, 1), 0.0)
+                through = through + pltpu.roll(through, shift, 1)
+                step *= 2
+            before = inner - x
+        through = through.reshape(some, steps, 8, 128)
+        before = before.reshape(some, steps, 8, 128)
+        run = through[:, 0]
+        out = [before[:, 0]]
+        for i in range(1, steps):
             out.append(before[:, i] + run)
             run = run + through[:, i]
         return jnp.stack(out, axis=1), run
 
     def wide(x):
-        return x.reshape(tiles, 1, 8, 128)
-
-    def full(x):
-        return x.reshape(tiles, steps, 8, 128)
+        return x.reshape(some, 1, 8, 128)
+
+    def full(x, c):
+        return x[c * rows : c * rows + rows].reshape(some, steps, 8, x.shape[1])
+
+    def slots(x, c):
+        return x.reshape(tiles, 8, 128)[c * some : c * some + some]
+
+    def joined(parts):
+        return jnp.concatenate([x.reshape(some * 8, 128) for x in parts], axis=0)
+
+    def pairs(x):
+        return paired(x.reshape(rows, 128))
 
     mark_col = marks_t.reshape(tiles, width, 1)[:, 0:8, :].reshape(small, 1)
     square = (small, small)
@@ -349,35 +373,55 @@
     ahead = jnp.concatenate([ahead, ahead], axis=1)
     behind = jnp.concatenate([behind, behind], axis=1)
 
-    z = dot16(u0_t, basis3) - OFFSET
-    filled = marks_t > 0.0
-    tail = jnp.exp(-jnp.abs(z))
-    alpha = jnp.where(filled, jnp.where(z >= 0.0, 1.0, tail) / (1.0 + tail), 0.0)
-    clear = jnp.where(filled, -(jnp.maximum(z, 0.0) + jnp.log1p(tail)), 0.0)
-    before, through = scan(clear)
-    before = before + wide(pick_left(ahead, through.reshape(small, 128)))
-    visible = full(alpha) * jnp.exp(before)
-    visible_pair = paired(visible.reshape(places, 128))
-    alpha = full(alpha)
-    rest = 1.0 - alpha
+    z_all = dot16(u0_t, basis3) - OFFSET
+    alpha, before, through = [], [], []
+    for c in range(chunks):
+        z = full(z_all, c)
+        filled = full(marks_t, c) > 0.0
+        tail = jnp.exp(-jnp.abs(z))
+        alpha.append(jnp.where(filled, jnp.where(z >= 0.0, 1.0, tail) / (1.0 + tail), 0.0))
+        clear = jnp.where(filled, -(jnp.maximum(z, 0.0) + jnp.log(1.0 + tail)), 0.0)
+        inner, whole = scan(clear)
+        before.append(inner)
+        through.append(whole)
+    front = pick_left(ahead, joined(through))
+    visible = [
+        alpha[c] * jnp.exp(before[c] + wide(slots(front, c))) for c in range(chunks)
+    ]
+    visible_pair = jnp.concatenate([pairs(x) for x in visible], axis=0)
 
     def image_tangent(parts):
         du = jnp.concatenate(parts, axis=1)
-        dz = full(dot16(turned3(parts), basis3))
-        before, through = scan(-alpha * dz)
-        before = before + wide(pick_left(ahead, through.reshape(small, 128)))
-        moved = visible * (rest * dz + before)
-        return wide_dot(du, visible_pair) + wide_dot(u0, paired(moved.reshape(places, 128)))
+        dz_all = dot16(turned3(parts), basis3)
+        before, through, moved = [], [], []
+        for c in range(chunks):
+            inner, whole = scan(-alpha[c] * full(dz_all, c))
+            before.append(inner)
+            through.append(whole)
+        front = pick_left(ahead, joined(through))
+        for c in range(chunks):
+            shift = before[c] + wide(slots(front, c))
+            moved.append(
+                pairs(visible[c] * ((1.0 - alpha[c]) * full(dz_all, c) + shift))
+            )
+        return wide_dot(du, visible_pair) + wide_dot(u0, jnp.concatenate(moved, axis=0))
 
     def cotangent(image, buf):
         image = jnp.where(color_row, image, 0.0)
         pull = image * weight
         energy = jnp.broadcast_to(total(pull * image), (1, 128))
-        h = full(dot16(u0_t, three_b(pull))) * visible
-        before, through = scan(h)
-        later = through + pick_left(behind, through.reshape(small, 128)).reshape(tiles, 8, 128)
-        z_bar = h * rest - alpha * (wide(later) - before - h)
-        u_bar = wide_dot_t(basis, paired(z_bar.reshape(places, 128))) + wide_dot_t(
+        h_all = dot16(u0_t, three_b(pull))
+        h, before, through, z_bar = [], [], [], []
+        for c in range(chunks):
+            h.append(full(h_all, c) * visible[c])
+            inner, whole = scan(h[c])
+            before.append(inner)
+            through.append(whole)
+        back = pick_left(behind, joined(through))
+        for c in range(chunks):
+            later = wide(through[c] + slots(back, c)) - before[c] - h[c]
+            z_bar.append(pairs(h[c] * (1.0 - alpha[c]) - alpha[c] * later))
+        u_bar = wide_dot_t(basis, jnp.concatenate(z_bar, axis=0)) + wide_dot_t(
             pull, visible_pair
         )
         put(buf, 0, swapped(u_bar))
@@ -431,12 +475,14 @@
     to_owners(b2_send, b2_recv, 4)
 
     direction = residual + beta * right
+    res_ref[...] = residual
     landed(b2_recv, everyone - 1, 4)
     product, energy = parameters(b2_recv)
     product = product + damp * direction
     step2 = rr1 / (energy + sds + 2.0 * beta * sdr + beta * beta * rdr)
-    sol_ref[...] = step1 * right + step2 * direction
-    res_ref[...] = residual - step2 * product
+    change_ref[...] = step2 * product
+    coef1_ref[...] = jnp.broadcast_to(step1 + step2 * beta, (1, gauss))
+    coef2_ref[...] = jnp.broadcast_to(step2, (1, gauss))
 
     if views > 1:
         left(xbuf, views - 1, 0)
@@ -469,11 +515,12 @@
         shape = jax.ShapeDtypeStruct(linear_point.shape, F32)
         vmem = pl.BlockSpec(memory_space=pltpu.VMEM)
         first, later = 2 * depth + 1, depth + 1
-        return pl.pallas_call(
+        coef = jax.ShapeDtypeStruct((1, gauss), F32)
+        middle, change, coef1, coef2 = pl.pallas_call(
             functools.partial(kernel, views, tiles),
-            out_shape=(shape, shape),
+            out_shape=(shape, shape, coef, coef),
             in_specs=[pl.BlockSpec(memory_space=pltpu.HBM)] * 9,
-            out_specs=(vmem, vmem),
+            out_specs=(vmem,) * 4,
             scratch_shapes=[
                 pltpu.VMEM((views, gauss, tiles * width), BF16),
                 pltpu.VMEM((views, FEATS + 8, 128), F32),
@@ -496,6 +543,7 @@
                 collective_id=0, has_side_effects=True, vmem_limit_bytes=63 * 1024 * 1024
             ),
         )(*args)
+        return coef1 * right_side + coef2 * middle, middle - change
 
     in_specs = (
         P(None, "tiles"),

time: 34 us -> 34 us (level)
  other arithmetic: 0 us -> 1.7 us
  local copies, waits for them, and re-layouts: 2.26 us -> 0.67 us
    sub x0 -> x1, other arithmetic: none -> 1.7 us  [body(): return (coef1 * right_side + coef2 * middle, middle - change)]
    unnamed x4 -> x6, local copies, waits for them, and re-layouts: 2.26 us -> 0.67 us
where the time goes in v2:
time: 34 us; the launch traced here: 33.8 us
  Pallas kernels  30.8 us (91%)
  other arithmetic  1.7 us (5%)
  local copies, waits for them, and re-layouts  0.67 us (2%)
  between operations  0.67 us (2%)
    pallas_call x1, Pallas kernels, body(): pl.pallas_call(functools.partial(kernel, views, tiles), out_shape=(shape,...  30.8 us
    sub x1, other arithmetic, body(): return (coef1 * right_side + coef2 * middle, middle - change)  1.7 us

profile of v2, /device:TPU:0, one launch (start us, length us, event | category | flops | bytes accessed | tf_op | source)
XLA Modules:
  0.0 33.8 jit_solution(4096198600491683141)
XLA Ops:
  0.6 0.0 copy-start
  0.6 30.8 %shard_map.104 = (f32[59,512]{1,0:T(8,128)}, f32[59,512]{1,0:T(8,128)}, f32[1,512]{1,0:T(1,128)}, f32[1,512]{1,0:T(1,128)}) custom-call(f32[59,512]{1,0:T(8,128)} %refs_0_.1, f32[59,512]{1,0:T(8,128)} %refs_1_.1, f32[59,512]{1,0:T(8,128)} %refs_2_.1, f32[16,59]{1,0:T(8,128)} %bitcast.9, f32[12,1,128]{2,1,0:T(1,128)} %bitcast.10, f32[1,128]{1,0:T(1,128)} %bitcast.14, ...), custom_call_target="tpu_custom_call" | custom-call | tf_op jit(solution)/shard_map/pallas_call | solution.py:519
  31.4 0.0 copy-start.2
  31.4 0.0 copy-start.1
  31.4 0.0 copy-done
  31.4 0.6 %copy-done.2 = f32[1,512]{1,0:T(1,128)S(1)} copy-done((f32[1,512]{1,0:T(1,128)S(1)}, f32[1,512]{1,0:T(1,128)}, u32[]{:S(2)}) %copy-start.2) | copy-done | bytes 2072
  32.1 0.0 copy-done.1
  32.1 1.7 %fusion = (f32[59,512]{1,0:T(8,128)}, f32[59,512]{1,0:T(8,128)}) fusion(f32[59,512]{1,0:T(8,128)} %get-tuple-element.8, f32[59,512]{1,0:T(8,128)} %get-tuple-element.9, f32[512]{0:T(512)S(1)} %bitcast.13, f32[59,512]{1,0:T(8,128)S(1)} %copy-done, f32[512]{0:T(512)S(1)} %bitcast.12), kind=kLoop, calls=%fused_computation.1 | loop fusion | flops 120832 | bytes 608256 | tf_op jit(solution)/shard_map/sub | solution.py:546
Async XLA Ops:
  0.6 30.8 %copy-start = (f32[59,512]{1,0:T(8,128)S(1)}, f32[59,512]{1,0:T(8,128)}, u32[]{:S(2)}) copy-start(f32[59,512]{1,0:T(8,128)} %refs_1_.1) | copy-start | bytes 362500
  31.4 0.7 %copy-start.2 = (f32[1,512]{1,0:T(1,128)S(1)}, f32[1,512]{1,0:T(1,128)}, u32[]{:S(2)}) copy-start(f32[1,512]{1,0:T(1,128)} %get-tuple-element.7) | copy-start | bytes 6148
  31.4 0.7 %copy-start.1 = (f32[1,512]{1,0:T(1,128)S(1)}, f32[1,512]{1,0:T(1,128)}, u32[]{:S(2)}) copy-start(f32[1,512]{1,0:T(1,128)} %get-tuple-element.6) | copy-start | bytes 6148

commit v3 on v2

v3 whole, which is shorter than its diff:
```python
import functools

import jax
import jax.numpy as jnp
from jax import lax
from jax.experimental import pallas as pl
from jax.experimental.pallas import tpu as pltpu
from jax.sharding import PartitionSpec as P

MESH = pl.DeviceIdType.MESH
F32 = jnp.float32
BF16 = jnp.bfloat16
FEATS = 16
ITERS = 2
OFFSET = 6.0


def dot16(a, b, dims=((1,), (0,))):
    return lax.dot_general(a, b, (dims, ((), ())), preferred_element_type=F32)


def split(x):
    high = x.astype(BF16)
    return high, (x - high.astype(F32)).astype(BF16)


def stacked(x):
    return jnp.concatenate(split(x), axis=0)


def halves_sum(x):
    rows = x.shape[0] // 2
    return x[:rows] + x[rows:]


def pick(x, onehot, dims=((1,), (0,))):
    return halves_sum(dot16(stacked(x), onehot, dims))


def pick_left(twice, x):
    return dot16(twice, stacked(x))


def small_dot(a, b):
    high, low = split(b)
    left = stacked(a)
    return halves_sum(dot16(left, high)) + dot16(left[: a.shape[0]], low)


def wide_dot(a, pair):
    return halves_sum_wide(dot16(stacked(a), pair))


def halves_sum_wide(x):
    rows, lanes = x.shape[0] // 2, x.shape[1] // 2
    return x[:rows, :lanes] + x[rows:, :lanes] + x[:rows, lanes:]


def paired(x):
    return jnp.concatenate(split(x), axis=1)


def wide_dot_t(a, pair):
    high, low = split(a)
    left = jnp.concatenate(
        [
            jnp.concatenate([high, high], axis=1),
            jnp.concatenate([low, jnp.zeros_like(low)], axis=1),
        ],
        axis=0,
    )
    return halves_sum(dot16(left, pair, ((1,), (1,))))


def three_a(x):
    high, low = split(x)
    return jnp.concatenate([high, high, low], axis=0)


def three_b(x):
    high, low = split(x)
    return jnp.concatenate([high, low, high], axis=0)


def iota(shape, axis):
    return lax.broadcasted_iota(jnp.int32, shape, axis)


def total(x):
    return jnp.sum(jnp.sum(x, axis=0, keepdims=True), axis=1, keepdims=True)


def swap_blocks(x, width):
    groups = 128 // width
    depth = FEATS // groups
    rows, lanes = iota(x.shape, 0), iota(x.shape, 1)
    bit = 1
    while bit < groups:
        up, over = depth * bit, width * bit
        row_bit = (rows // up) % 2
        lane_bit = (lanes // over) % 2
        down = pltpu.roll(pltpu.roll(x, FEATS - up, 0), over, 1)
        back = pltpu.roll(pltpu.roll(x, up, 0), 128 - over, 1)
        x = jnp.where(row_bit == lane_bit, x, jnp.where(lane_bit == 1, down, back))
        bit *= 2
    return x


def kernel(
    views,
    tiles,
    *refs,
):
    my_view = lax.axis_index("views")
    me = lax.axis_index("tiles")
    flat = my_view * tiles + me
    everyone = views * tiles
    inputs, refs = refs[:9], refs[9:]
    sol_ref, res_ref, onehot, xbuf = refs[:4]
    p_send, p_recv, f_send, f_recv, b_send, b_recv = refs[4:10]
    tile_state, owner_state, held = refs[10:18], refs[18], refs[19:28]
    alpha_ref, visible_ref, pair_ref, u0_ref, u0t_ref, ahead_ref, behind_ref, image_ref = tile_state
    direction_ref = owner_state
    send_sem, recv_sem, in_sem = refs[28:]
    lp_ref, rs_ref, dm_ref, proj_ref, basis_ref, weight_ref, order_ref, dest_ref, depth_ref = held
    fetches = [
        pltpu.make_async_copy(inputs[i], held[i], in_sem.at[i]) for i in range(9)
    ]
    for i in (6, 7, 8, 3, 1, 0, 2, 4, 5):
        fetches[i].start()
    count = dest_ref.shape[1]
    gauss = order_ref.shape[1]
    params = rs_ref.shape[0]
    per = gauss // count
    capacity = max(2, count // tiles)
    width = per * capacity
    places = tiles * width
    blocks = places // 128
    groups = 128 // width
    depth = FEATS // groups

    barrier = pltpu.get_barrier_semaphore()

    def greet(k, carry):
        other = lax.rem(flat + k, everyone)
        pl.semaphore_signal(
            barrier, inc=1, device_id=(other // tiles, lax.rem(other, tiles)), device_id_type=MESH
        )
        return carry

    lax.fori_loop(1, everyone, greet, 0)

    eye = iota((count, count), 0) == iota((count, count), 1)
    for i in (6, 7, 8):
        fetches[i].wait()
    dest_row = dest_ref[...].astype(F32)
    dest = jnp.sum(jnp.where(eye, dest_row, 0.0), axis=1, keepdims=True)
    earlier = iota((count, count), 1) < iota((count, count), 0)
    position = jnp.sum(
        jnp.where((dest_row == dest) & earlier, 1.0, 0.0), axis=1, keepdims=True
    )
    slot = dest * float(capacity) + position
    mark = jnp.sum(jnp.where(eye, depth_ref[...].astype(F32), 0.0), axis=1, keepdims=True) + 1.0
    order = order_ref[...]
    own = iota((count, gauss), 1) // per == iota((count, gauss), 0)
    high = jnp.where(own, (order // 256).astype(F32), 0.0)
    low = jnp.where(own, (order % 256).astype(F32), 0.0)
    spread = (
        iota((gauss, 128), 0) % per == (iota((gauss, 128), 1) % width) // capacity
    ).astype(F32).astype(BF16)
    listed = dot16(jnp.concatenate([high, low], axis=0).astype(BF16), spread)
    listed = listed[:count] * 256.0 + listed[count:] + 1.0
    ids, marks = [], []
    for k in range(blocks):
        lane = iota((count, 128), 1) + k * 128
        wanted = (lane // width) * capacity + lane % capacity
        here = slot == wanted.astype(F32)
        ids.append(jnp.sum(jnp.where(here, listed, 0.0), axis=0, keepdims=True) - 1.0)
        marks.append(jnp.sum(jnp.where(here, mark, 0.0), axis=0, keepdims=True))

    def place_matrix(rows):
        numbers = iota((gauss, 128), 0).astype(F32)
        return jnp.concatenate(
            [(numbers == row).astype(F32).astype(BF16) for row in rows], axis=1
        )

    mine = place_matrix(ids)
    onehot[my_view] = mine
    for i in (3, 1, 0, 2, 4, 5):
        fetches[i].wait()
    proj = proj_ref[...]
    xbuf[my_view, 0:FEATS, 0:params] = proj
    for k in range(blocks):
        xbuf[my_view, FEATS + k : FEATS + 1 + k, :] = ids[k]

    u_primal = pick(small_dot(proj, lp_ref[...]), mine)
    lane = iota((1, 128), 1)

    def put(buf, parts, extra):
        for k in range(blocks):
            for j in range(groups):
                t = k * groups + j
                buf[t, 0:depth, :] = parts[k][j * depth : j * depth + depth]
                buf[t, depth : depth + 1, :] = extra[t]

    def swapped(u):
        return [swap_blocks(u[:, k * 128 : k * 128 + 128], width) for k in range(blocks)]

    top = iota((FEATS, 128), 0) == 0
    extra = []
    for k in range(blocks):
        ranks = swap_blocks(jnp.where(top, marks[k], 0.0), width)
        extra += [ranks[j * depth : j * depth + 1] for j in range(groups)]
    put(p_send, swapped(u_primal), extra)
    res_ref[...] = rs_ref[...]
    sol_ref[...] = jnp.zeros_like(sol_ref)
    direction_ref[...] = jnp.zeros_like(direction_ref)
    image_ref[...] = jnp.zeros_like(image_ref)

    pl.semaphore_wait(barrier, everyone - 1)

    def send(src, dst, view, tile, sem):
        return pltpu.make_async_remote_copy(
            src_ref=src,
            dst_ref=dst,
            send_sem=send_sem.at[sem],
            recv_sem=recv_sem.at[sem],
            device_id=(view, tile),
            device_id_type=MESH,
        )

    def part(buf, number):
        return buf.at[number, pl.ds(0, depth + 1)]

    def to_tiles(src, dst, sem):
        def step(k, carry):
            other = lax.rem(me + k, tiles)
            send(part(src, other), part(dst, me), my_view, other, sem).start()
            return carry

        lax.fori_loop(1, tiles, step, 0)
        dst[me] = src[me]

    def to_owners(src, dst, sem):
        def step(k, carry):
            other = lax.rem(flat + k, everyone)
            tile = lax.rem(other, tiles)
            send(part(src, tile), part(dst, flat), other // tiles, tile, sem).start()
            return carry

        lax.fori_loop(1, everyone, step, 0)
        dst[flat] = src[me]

    def landed(dst, number, sem):
        whole = dst.at[pl.ds(0, number), pl.ds(0, depth + 1)]
        send(whole, whole, my_view, me, sem).wait_recv()

    def left(src, number, sem):
        whole = src.at[pl.ds(0, number), pl.ds(0, depth + 1)]
        send(whole, whole, my_view, me, sem).wait_send()

    to_tiles(p_send, p_recv, 1)
    for k in range(1, views):
        send(xbuf.at[my_view], xbuf.at[my_view], lax.rem(my_view + k, views), me, 0).start()

    basis = jnp.concatenate(
        [jnp.ones((1, 128), F32), jnp.zeros((3, 128), F32)]
        + [basis_ref[i] for i in range(FEATS - 4)],
        axis=0,
    )
    basis3 = three_b(basis)
    weight = weight_ref[...]
    color_row = (iota((FEATS, 128), 0) >= 1) & (iota((FEATS, 128), 0) <= 3)

    def gathered(buf, first):
        out = []
        for k in range(blocks):
            lines = [buf[first + k * groups + j, 0:depth, :] for j in range(groups)]
            out.append(swap_blocks(jnp.concatenate(lines, axis=0), width))
        return out

    def turned(parts):
        return jnp.concatenate([part.T for part in parts], axis=0)

    def turned3(parts):
        return turned([three_a(part).astype(F32) for part in parts]).astype(BF16)

    def lanes_total(buf, row, number):
        return jnp.sum(buf[0:number], axis=0)[row : row + 1]

    halves = 8 // capacity
    steps = width // 8
    small = tiles * 8
    some = 4
    chunks = tiles // some
    rows = some * width
    sub = iota((some * steps, 8, 128), 1)

    def scan(x):
        x = x.reshape(some * steps, 8, 128)
        if halves == 2:
            moved = pltpu.roll(x, capacity, 1)
            before = jnp.where(sub >= capacity, moved, 0.0)
            through = x + moved
        else:
            through = inner = x
            step = 1
            while step < halves:
                shift = step * capacity
                inner = inner + jnp.where(sub >= shift, pltpu.roll(inner, shift, 1), 0.0)
                through = through + pltpu.roll(through, shift, 1)
                step *= 2
            before = inner - x
        through = through.reshape(some, steps, 8, 128)
        before = before.reshape(some, steps, 8, 128)
        run = through[:, 0]
        out = [before[:, 0]]
        for i in range(1, steps):
            out.append(before[:, i] + run)
            run = run + through[:, i]
        return jnp.stack(out, axis=1), run

    def wide(x):
        return x.reshape(some, 1, 8, 128)

    def full(x, c):
        return x[c * rows : c * rows + rows].reshape(some, steps, 8, x.shape[1])

    def slots(x, c):
        return x.reshape(tiles, 8, 128)[c * some : c * some + some]

    def joined(parts):
        return jnp.concatenate([x.reshape(some * 8, 128) for x in parts], axis=0)

    def pairs(x):
        return paired(x.reshape(rows, 128))

    def primal():
        landed(p_recv, tiles - 1, 1)
        primal_parts = gathered(p_recv, 0)
        u0 = jnp.concatenate(primal_parts, axis=1)
        u0_ref[...] = u0
        u0_t = turned3(primal_parts)
        u0t_ref[...] = u0_t
        ranks = []
        for k in range(blocks):
            lines = []
            for j in range(groups):
                lines.append(p_recv[k * groups + j, depth : depth + 1, :])
                lines.append(jnp.zeros((depth - 1, 128), F32))
            ranks.append(swap_blocks(jnp.concatenate(lines, axis=0), width))
        marks_t = turned(ranks)[:, 0:1]
        mark_col = marks_t.reshape(tiles, width, 1)[:, 0:8, :].reshape(small, 1)
        square = (small, small)
        mark_row = jnp.sum(
            jnp.where(iota(square, 0) == iota(square, 1), mark_col, 0.0), axis=0, keepdims=True
        )
        first = (iota(square, 1) % 8) < capacity
        ahead = (first & (mark_row < mark_col) & (mark_row > 0.0)).astype(F32).astype(BF16)
        behind = (first & (mark_row > mark_col)).astype(F32).astype(BF16)
        ahead = jnp.concatenate([ahead, ahead], axis=1)
        ahead_ref[...] = ahead
        behind_ref[...] = jnp.concatenate([behind, behind], axis=1)

        z_all = dot16(u0_t, basis3) - OFFSET
        alpha, before, through = [], [], []
        for c in range(chunks):
            z = full(z_all, c)
            filled = full(marks_t, c) > 0.0
            tail = jnp.exp(-jnp.abs(z))
            alpha.append(jnp.where(filled, jnp.where(z >= 0.0, 1.0, tail) / (1.0 + tail), 0.0))
            clear = jnp.where(filled, -(jnp.maximum(z, 0.0) + jnp.log(1.0 + tail)), 0.0)
            inner, whole = scan(clear)
            before.append(inner)
            through.append(whole)
        front = pick_left(ahead, joined(through))
        for c in range(chunks):
            seen = alpha[c] * jnp.exp(before[c] + wide(slots(front, c)))
            alpha_ref[c] = alpha[c]
            visible_ref[c] = seen
            pair_ref[c * rows : c * rows + rows, :] = pairs(seen)

    def image_tangent(parts):
        du = jnp.concatenate(parts, axis=1)
        dz_all = dot16(turned3(parts), basis3)
        before, through, moved = [], [], []
        for c in range(chunks):
            inner, whole = scan(-alpha_ref[c] * full(dz_all, c))
            before.append(inner)
            through.append(whole)
        front = pick_left(ahead_ref[...], joined(through))
        for c in range(chunks):
            shift = before[c] + wide(slots(front, c))
            moved.append(
                pairs(visible_ref[c] * ((1.0 - alpha_ref[c]) * full(dz_all, c) + shift))
            )
        return wide_dot(du, pair_ref[...]) + wide_dot(u0_ref[...], jnp.concatenate(moved, axis=0))

    def cotangent(image, buf):
        image = jnp.where(color_row, image, 0.0)
        pull = image * weight
        energy = jnp.broadcast_to(total(pull * image), (1, 128))
        h_all = dot16(u0t_ref[...], three_b(pull))
        h, before, through, z_bar = [], [], [], []
        for c in range(chunks):
            h.append(full(h_all, c) * visible_ref[c])
            inner, whole = scan(h[c])
            before.append(inner)
            through.append(whole)
        back = pick_left(behind_ref[...], joined(through))
        for c in range(chunks):
            later = wide(through[c] + slots(back, c)) - before[c] - h[c]
            z_bar.append(pairs(h[c] * (1.0 - alpha_ref[c]) - alpha_ref[c] * later))
        u_bar = wide_dot_t(basis, jnp.concatenate(z_bar, axis=0)) + wide_dot_t(
            pull, pair_ref[...]
        )
        put(buf, swapped(u_bar), [energy] * tiles)

    def parameters(buf):
        left, right = [], []
        for v in range(views):
            u_bar = jnp.concatenate(gathered(buf, v * tiles), axis=1)
            left.append(three_a(xbuf[v, 0:FEATS, :]))
            right.append(three_b(pick(u_bar, onehot[v], ((1,), (1,)))))
        out = dot16(
            jnp.concatenate(left, axis=0), jnp.concatenate(right, axis=0), ((0,), (0,))
        )
        return out[:params], lanes_total(buf, depth, everyone)[:, 0:1]

    def other_views():
        whole = xbuf.at[pl.ds(0, views - 1)]
        send(whole, whole, my_view, me, 0).wait_recv()
        for k in range(1, views):
            other = lax.rem(my_view + k, views)
            onehot[other] = place_matrix(
                [xbuf[other, FEATS + b : FEATS + 1 + b, :] for b in range(blocks)]
            )

    def iterate(turn, carry):
        rr_old, old_damped = carry
        residual = res_ref[...]
        u = swapped(pick(small_dot(proj, residual), onehot[my_view]))
        damped_residual = dm_ref[...] * residual
        sums = (
            jnp.where(lane == 0, total(residual * residual), 0.0)
            + jnp.where(lane == 1, total(damped_residual * residual), 0.0)
            + jnp.where(lane == 2, total(damped_residual * direction_ref[...]), 0.0)
        )
        put(f_send.at[turn], u, [sums] * tiles)
        to_tiles(f_send.at[turn], f_recv.at[turn], 2 + turn)

        @pl.when(turn == 0)
        def _():
            primal()

        landed(f_recv.at[turn], tiles - 1, 2 + turn)
        sums = lanes_total(f_recv.at[turn], depth, tiles)
        rr = sums[:, 0:1]
        beta = jnp.where(turn == 0, 0.0, rr / rr_old)
        image = image_tangent(gathered(f_recv.at[turn], 0)) + beta * image_ref[...]
        image_ref[...] = image
        cotangent(image, b_send.at[turn])
        to_owners(b_send.at[turn], b_recv.at[turn], 2 + ITERS + turn)
        direction = residual + beta * direction_ref[...]
        direction_ref[...] = direction
        both_damped = sums[:, 1:2] + 2.0 * beta * sums[:, 2:3] + beta * beta * old_damped
        if views > 1:
            pl.when(turn == 0)(other_views)

        landed(b_recv.at[turn], everyone - 1, 2 + ITERS + turn)
        product, energy = parameters(b_recv.at[turn])
        product = product + dm_ref[...] * direction
        step = rr / (energy + both_damped)
        sol_ref[...] += step * direction
        res_ref[...] = residual - step * product
        return rr, both_damped

    lax.fori_loop(0, ITERS, iterate, (jnp.ones((1, 1), F32), jnp.zeros((1, 1), F32)))

    if views > 1:
        whole = xbuf.at[pl.ds(0, views - 1)]
        send(whole, whole, my_view, me, 0).wait_send()
    left(p_recv, tiles - 1, 1)
    for turn in range(ITERS):
        left(f_recv.at[turn], tiles - 1, 2 + turn)
        left(b_recv.at[turn], everyone - 1, 2 + ITERS + turn)


def store(a_ref, b_ref, a_out, b_out, a_held, b_held, sem):
    rows = a_ref.shape[0]
    half = rows // 16 * 8
    parts = []
    for src, mid, out in ((a_ref, a_held, a_out), (b_ref, b_held, b_out)):
        for place in (pl.ds(0, half), pl.ds(half, rows - half)):
            number = len(parts)
            parts.append(
                (
                    pltpu.make_async_copy(src.at[place], mid.at[place], sem.at[0, number]),
                    pltpu.make_async_copy(mid.at[place], out.at[place], sem.at[1, number]),
                )
            )
    for come, go in parts:
        come.start()
    for come, go in parts:
        come.wait()
        go.start()
    for come, go in parts:
        go.wait()


def solution(mesh):
    views, tiles = mesh.shape["views"], mesh.shape["tiles"]

    def body(*args):
        linear_point, right_side, damping, proj, basis, weight, order, dest, depths = args
        gauss, count = order.shape[2], dest.shape[1]
        capacity = max(2, count // tiles)
        width = gauss // count * capacity
        depth = FEATS * width // 128
        args = (
            linear_point,
            right_side,
            damping,
            jnp.swapaxes(proj[0], 0, 1),
            jnp.swapaxes(basis[0], 0, 1),
            weight[0],
            order[0],
            dest.reshape(1, count),
            depths,
        )
        shape = jax.ShapeDtypeStruct(linear_point.shape, F32)
        vmem = pl.BlockSpec(memory_space=pltpu.VMEM)
        places = tiles * width
        message = (8, 128)
        chunk = (tiles // 4, 4, width // 8, 8, 128)
        results = pl.pallas_call(
            functools.partial(kernel, views, tiles),
            out_shape=(shape, shape),
            in_specs=[pl.BlockSpec(memory_space=pltpu.HBM)] * 9,
            out_specs=(vmem, vmem),
            scratch_shapes=[
                pltpu.VMEM((views, gauss, places), BF16),
                pltpu.VMEM((views, FEATS + 8, 128), F32),
                pltpu.VMEM((tiles,) + message, F32),
                pltpu.VMEM((tiles,) + message, F32),
                pltpu.VMEM((ITERS, tiles) + message, F32),
                pltpu.VMEM((ITERS, tiles) + message, F32),
                pltpu.VMEM((ITERS, tiles) + message, F32),
                pltpu.VMEM((ITERS, views * tiles) + message, F32),
                pltpu.VMEM(chunk, F32),
                pltpu.VMEM(chunk, F32),
                pltpu.VMEM((places, 256), BF16),
                pltpu.VMEM((FEATS, places), F32),
                pltpu.VMEM((places, 3 * FEATS), BF16),
                pltpu.VMEM((tiles * 8, tiles * 16), BF16),
                pltpu.VMEM((tiles * 8, tiles * 16), BF16),
                pltpu.VMEM((FEATS, 128), F32),
                pltpu.VMEM(linear_point.shape, F32),
            ]
            + [pltpu.VMEM(arg.shape, arg.dtype) for arg in args]
            + [
                pltpu.SemaphoreType.DMA((2 + 2 * ITERS,)),
                pltpu.SemaphoreType.DMA((2 + 2 * ITERS,)),
                pltpu.SemaphoreType.DMA((9,)),
            ],
            compiler_params=pltpu.CompilerParams(
                collective_id=0, has_side_effects=True, vmem_limit_bytes=63 * 1024 * 1024
            ),
        )(*args)
        return pl.pallas_call(
            store,
            out_shape=(shape, shape),
            in_specs=[pl.BlockSpec(memory_space=pltpu.HBM)] * 2,
            out_specs=(pl.BlockSpec(memory_space=pltpu.HBM),) * 2,
            scratch_shapes=[
                pltpu.VMEM(shape.shape, F32),
                pltpu.VMEM(shape.shape, F32),
                pltpu.SemaphoreType.DMA((2, 4)),
            ],
            compiler_params=pltpu.CompilerParams(vmem_limit_bytes=63 * 1024 * 1024),
        )(*results)

    in_specs = (
        P(None, "tiles"),
        P(None, "tiles"),
        P(None, "tiles"),
        P("views", None, None),
        P("views", "tiles", None, None),
        P("views", "tiles", None),
        P("views", "tiles", None),
        P("views", "tiles", None),
        P("views", "tiles"),
    )
    out_specs = (P(None, "tiles"), P(None, "tiles"))
    return jax.shard_map(body, mesh=mesh, in_specs=in_specs, out_specs=out_specs, check_vma=False)
```

time: 34 us -> 33.6 us (0.988)
  Pallas kernels: 30.8 us -> 32.8 us
  other arithmetic: 1.7 us -> 0 us
  local copies, waits for them, and re-layouts: 0.67 us -> 0 us
    sub x1 -> x0, other arithmetic: 1.7 us -> none  [body(): return (coef1 * right_side + coef2 * middle, middle - change)]
    pallas_call x0 -> x1, Pallas kernels: none -> 1.69 us  [body(): pl.pallas_call(store, out_shape=(shape, shape), in_specs=[pl.BlockSpec(me...]
    unnamed x6 -> x0, local copies, waits for them, and re-layouts: 0.67 us -> none
where the time goes in v3:
time: 33.6 us; the launch traced here: 33.4 us
  Pallas kernels  32.8 us (98%)
  between operations  0.64 us (2%)
    pallas_call x1, Pallas kernels, body(): pl.pallas_call(functools.partial(kernel, views, tiles), out_shape=(shape,...  31.1 us
    pallas_call x1, Pallas kernels, body(): pl.pallas_call(store, out_shape=(shape, shape), in_specs=[pl.BlockSpec(me...  1.69 us

profile of v3, /device:TPU:0, one launch (start us, length us, event | category | flops | bytes accessed | tf_op | source)
XLA Modules:
  0.0 33.4 jit_solution(11204367038982268641)
XLA Ops:
  0.6 31.1 %shard_map.104 = (f32[59,512]{1,0:T(8,128)}, f32[59,512]{1,0:T(8,128)}) custom-call(f32[59,512]{1,0:T(8,128)} %refs_0_.1, f32[59,512]{1,0:T(8,128)} %refs_1_.1, f32[59,512]{1,0:T(8,128)} %refs_2_.1, f32[16,59]{1,0:T(8,128)} %bitcast.7, f32[12,1,128]{2,1,0:T(1,128)} %bitcast.8, f32[1,128]{1,0:T(1,128)} %bitcast.10, s32[1,512]{1,0:T(1,128)} %bitcast.9, ...), custom_call_target="tpu_custom_call" | custom-call | tf_op jit(solution)/shard_map/pallas_call | solution.py:536
  31.7 1.7 %shard_map.105 = (f32[59,512]{1,0:T(8,128)}, f32[59,512]{1,0:T(8,128)}) custom-call(f32[59,512]{1,0:T(8,128)} %get-tuple-element.4.a_ref, f32[59,512]{1,0:T(8,128)} %get-tuple-element.5.b_ref), custom_call_target="tpu_custom_call" | custom-call | tf_op jit(solution)/shard_map/pallas_call | solution.py:570

commit v4 on v1

--- a/solution.py
+++ b/solution.py
@@ -229,23 +229,46 @@
             device_id_type=MESH,
         )
 
+    half = tiles // 2
+    far, near = (1 - me // half) * half, (me // half) * half
+
     def to_tiles(src, dst, sem):
-        def step(k, carry):
-            other = lax.rem(me + k, tiles)
+        def start(other):
             send(src.at[other], dst.at[me], my_view, other, sem).start()
+
+        def across(k, carry):
+            start(far + lax.rem(me + k, half))
             return carry
 
-        lax.fori_loop(1, tiles, step, 0)
+        def along(k, carry):
+            start(near + lax.rem(me + k, half))
+            return carry
+
+        lax.fori_loop(0, half, across, 0)
+        lax.fori_loop(1, half, along, 0)
         dst[me] = src[me]
 
     def to_owners(src, dst, sem):
-        def step(k, carry):
-            other = lax.rem(flat + k, everyone)
-            tile = lax.rem(other, tiles)
-            send(src.at[tile], dst.at[flat], other // tiles, tile, sem).start()
+        def start(view, tile):
+            send(src.at[tile], dst.at[flat], view, tile, sem).start()
+
+        def across(k, carry):
+            view = lax.rem(my_view + 1 + k // half, views)
+            start(view, far + lax.rem(me + k, half))
             return carry
 
-        lax.fori_loop(1, everyone, step, 0)
+        def beside(k, carry):
+            view = lax.rem(my_view + 1 + k // half, views)
+            start(view, near + lax.rem(me + k, half))
+            return carry
+
+        def along(k, carry):
+            start(my_view, near + lax.rem(me + k, half))
+            return carry
+
+        lax.fori_loop(0, views * half, across, 0)
+        lax.fori_loop(0, (views - 1) * half, beside, 0)
+        lax.fori_loop(1, half, along, 0)
         dst[flat] = src[me]
 
     def landed(dst, number, sem):
@@ -353,7 +376,7 @@
     filled = marks_t > 0.0
     tail = jnp.exp(-jnp.abs(z))
     alpha = jnp.where(filled, jnp.where(z >= 0.0, 1.0, tail) / (1.0 + tail), 0.0)
-    clear = jnp.where(filled, -(jnp.maximum(z, 0.0) + jnp.log1p(tail)), 0.0)
+    clear = jnp.where(filled, -(jnp.maximum(z, 0.0) + jnp.log(1.0 + tail)), 0.0)
     before, through = scan(clear)
     before = before + wide(pick_left(ahead, through.reshape(small, 128)))
     visible = full(alpha) * jnp.exp(before)
@@ -444,6 +467,28 @@
     left(b1_recv, everyone - 1, 2)
     left(f2_recv, tiles - 1, 3)
     left(b2_recv, everyone - 1, 4)
+
+
+def store(a_ref, b_ref, a_out, b_out, a_held, b_held, sem):
+    rows = a_ref.shape[0]
+    half = rows // 16 * 8
+    parts = []
+    for src, mid, out in ((a_ref, a_held, a_out), (b_ref, b_held, b_out)):
+        for place in (pl.ds(0, half), pl.ds(half, rows - half)):
+            number = len(parts)
+            parts.append(
+                (
+                    pltpu.make_async_copy(src.at[place], mid.at[place], sem.at[0, number]),
+                    pltpu.make_async_copy(mid.at[place], out.at[place], sem.at[1, number]),
+                )
+            )
+    for come, go in parts:
+        come.start()
+    for come, go in parts:
+        come.wait()
+        go.start()
+    for come, go in parts:
+        go.wait()
 
 
 def solution(mesh):
@@ -469,7 +514,7 @@
         shape = jax.ShapeDtypeStruct(linear_point.shape, F32)
         vmem = pl.BlockSpec(memory_space=pltpu.VMEM)
         first, later = 2 * depth + 1, depth + 1
-        return pl.pallas_call(
+        results = pl.pallas_call(
             functools.partial(kernel, views, tiles),
             out_shape=(shape, shape),
             in_specs=[pl.BlockSpec(memory_space=pltpu.HBM)] * 9,
@@ -496,6 +541,18 @@
                 collective_id=0, has_side_effects=True, vmem_limit_bytes=63 * 1024 * 1024
             ),
         )(*args)
+        return pl.pallas_call(
+            store,
+            out_shape=(shape, shape),
+            in_specs=[pl.BlockSpec(memory_space=pltpu.HBM)] * 2,
+            out_specs=(pl.BlockSpec(memory_space=pltpu.HBM),) * 2,
+            scratch_shapes=[
+                pltpu.VMEM(shape.shape, F32),
+                pltpu.VMEM(shape.shape, F32),
+                pltpu.SemaphoreType.DMA((2, 4)),
+            ],
+            compiler_params=pltpu.CompilerParams(vmem_limit_bytes=63 * 1024 * 1024),
+        )(*results)
 
     in_specs = (
         P(None, "tiles"),

time: 34 us -> 33.1 us (0.974)
  local copies, waits for them, and re-layouts: 2.26 us -> 0 us
  Pallas kernels: 30.9 us -> 32.3 us
    unnamed x4 -> x0, local copies, waits for them, and re-layouts: 2.26 us -> none
    pallas_call x0 -> x1, Pallas kernels: none -> 1.69 us  [body(): pl.pallas_call(store, out_shape=(shape, shape), in_specs=[pl.BlockSpec(me...]
where the time goes in v4:
time: 33.1 us; the launch traced here: 32.9 us
  Pallas kernels  32.3 us (98%)
  between operations  0.64 us (2%)
    pallas_call x1, Pallas kernels, body(): pl.pallas_call(functools.partial(kernel, views, tiles), out_shape=(shape,...  30.6 us
    pallas_call x1, Pallas kernels, body(): pl.pallas_call(store, out_shape=(shape, shape), in_specs=[pl.BlockSpec(me...  1.69 us

profile of v4, /device:TPU:0, one launch (start us, length us, event | category | flops | bytes accessed | tf_op | source)
XLA Modules:
  0.0 32.9 jit_solution(9015482504291273397)
XLA Ops:
  0.6 30.6 %shard_map.104 = (f32[59,512]{1,0:T(8,128)}, f32[59,512]{1,0:T(8,128)}) custom-call(f32[59,512]{1,0:T(8,128)} %refs_0_.1, f32[59,512]{1,0:T(8,128)} %refs_1_.1, f32[59,512]{1,0:T(8,128)} %refs_2_.1, f32[16,59]{1,0:T(8,128)} %bitcast.7, f32[12,1,128]{2,1,0:T(1,128)} %bitcast.8, f32[1,128]{1,0:T(1,128)} %bitcast.10, s32[1,512]{1,0:T(1,128)} %bitcast.9, ...), custom_call_target="tpu_custom_call" | custom-call | tf_op jit(solution)/shard_map/pallas_call | solution.py:517
  31.3 1.7 %shard_map.105 = (f32[59,512]{1,0:T(8,128)}, f32[59,512]{1,0:T(8,128)}) custom-call(f32[59,512]{1,0:T(8,128)} %get-tuple-element.4.a_ref, f32[59,512]{1,0:T(8,128)} %get-tuple-element.5.b_ref), custom_call_target="tpu_custom_call" | custom-call | tf_op jit(solution)/shard_map/pallas_call | solution.py:544
